TPU v7x, 32 devices: a whole 2x2x4 slice. The times are simulated.
32 devices in a mesh: band: 16 (over z, y, x), slab: 2 (over core).
Axes of the slice: x: 2, y: 2, z: 4, core: 2. Of those that a mesh axis runs over, the one named last changes fastest.
Arguments:
- feats: bfloat16 [2, 2048, 128], P('slab', 'band'), may hold values from -6 to 6
- nbrs: int32 [2, 2048, 16], P('slab', 'band'), may hold values from 0 to 2047
- w_pair: bfloat16 [128, 512], replicated, may hold values from -0.5 to 0.5
- stiff: float32 [4096], P('band'), may hold values from 0.5 to 2
- order: int32 [16], replicated, may hold values from 0 to 15, each once
Outputs:
- schur: float32 [2, 2048, 16, 256], P('slab', None, 'band')
- log_mean: float32 [], replicated
Inputs may be any that keep to these rules, and one draw needn't show every extreme that they name: `nbrs`: neighbours lie in the bead's own slab group. `order`: each column block appears once.
All inputs are finite; a program needn't handle non-finite values.
Results may differ from a plain program's by a relative error of at most 0.01.
Values may be sent and summed in bfloat16 or wider, within the bound.
A program may use at most 64 MiB of HBM per device.

v0:
```python
import math

import jax
import jax.numpy as jnp
from jax import lax
from jax.sharding import PartitionSpec as P

STEPS = 1


def from_root(block, axis, owner):
    block = jnp.where(lax.axis_index(axis) == owner, block, jnp.zeros_like(block))
    return lax.psum(block, axis)


def pair_factor(rows_feats, rows_nbrs, slab_feats, w_pair):
    count = rows_feats.shape[0]
    width = min(count, 128)
    blocks = count // width
    scale = 1.5 / math.sqrt(rows_nbrs.shape[1] * w_pair.shape[1])

    def one_block(pieces):
        own, links = pieces
        near = jnp.take(slab_feats, links, axis=0)
        mixed = (own[:, None, :].astype(jnp.float32) * near.astype(jnp.float32)).astype(
            jnp.bfloat16
        )
        pre = jnp.einsum("rne,ec->rnc", mixed, w_pair, preferred_element_type=jnp.float32)
        return (jnp.sum(jnp.tanh(pre), axis=1) * scale).astype(jnp.bfloat16)

    out = lax.map(
        one_block, (rows_feats.reshape(blocks, width, -1), rows_nbrs.reshape(blocks, width, -1))
    )
    return out.reshape(count, -1)


def on_device(feats, nbrs, w_pair, stiff, order):
    band_id = lax.axis_index("band")
    slab_id = lax.axis_index("slab")
    groups = lax.axis_size("slab")
    own_feats = feats[0]
    own_nbrs = nbrs[0]
    slab_feats = lax.all_gather(own_feats, "band", axis=0, tiled=True)
    own_factor = pair_factor(own_feats, own_nbrs, slab_feats, w_pair)
    slab_factor = lax.all_gather(own_factor, "band", axis=0, tiled=True)
    block = stiff.shape[0]
    count = slab_factor.shape[0]
    blocks_dev = count // block
    home = band_id // groups
    column_piece = lax.dynamic_slice_in_dim(slab_factor, home * block, block, 0)
    column_factor = from_root(column_piece, "slab", band_id % groups)
    matrix = jnp.einsum("qc,jc->qj", slab_factor, column_factor, preferred_element_type=jnp.float32)
    block_ids = jnp.arange(blocks_dev, dtype=jnp.int32) * groups + slab_id
    matrix = matrix.reshape(blocks_dev, block, block)
    matrix = matrix + jnp.where((block_ids == band_id)[:, None, None], jnp.diag(stiff), 0.0)
    identity = jnp.eye(block, dtype=jnp.float32)
    pivot = order[0]
    done = jnp.any(block_ids[:, None] == order[:1][None, :], axis=1)
    piece = lax.dynamic_index_in_dim(matrix, pivot // groups, 0, keepdims=False)
    pivot_block = from_root(piece.astype(jnp.bfloat16), "slab", pivot % groups).astype(piece.dtype)
    pivot_block = jnp.where(band_id == pivot, pivot_block, identity)
    lower = jnp.linalg.cholesky(pivot_block)
    solved = lax.linalg.triangular_solve(
        lower, matrix.reshape(count, block), left_side=False, lower=True, transpose_a=True
    )
    solved = jnp.where(done[:, None, None], 0.0, solved.reshape(blocks_dev, block, block))
    outgoing = solved.reshape(count, block).astype(jnp.bfloat16)
    panel = from_root(outgoing, "band", pivot)
    term = jnp.where(band_id == pivot, 2.0 * jnp.sum(jnp.log(jnp.diagonal(lower))), 0.0)
    mine = lax.dynamic_slice_in_dim(panel, home * block, block, 0)
    own_block = from_root(mine, "slab", band_id % groups)
    update = jnp.einsum("qk,jk->qj", panel, own_block, preferred_element_type=jnp.float32)
    matrix = matrix - update.reshape(blocks_dev, block, block)
    total = lax.psum(term, "band")
    schur = matrix.reshape(1, count, 1, block)
    return (schur, total / (STEPS * block))


def solution(mesh):
    in_specs = (P("slab", "band", None), P("slab", "band", None), P(), P("band"), P())
    out_specs = (P("slab", None, "band", None), P())
    return jax.shard_map(
        on_device, mesh=mesh, in_specs=in_specs, out_specs=out_specs, check_vma=False
    )
```

profile of v0, /device:TPU:0, one launch (start us, length us, event | category | flops | bytes accessed | tf_op | source)
XLA Modules:
  0.0 415.3 jit_solution(8127252810040491580)
XLA Ops:
  7.2 0.0 all-gather.3.cloned.1.call-start
  7.2 45.6 %all-gather = bf16[1,2048,128]{2,1,0:T(8,128)(2,1)S(1)} all-gather(bf16[1,128,128]{2,1,0:T(8,128)(2,1)} %param.5), channel_id=2, replica_groups=mesh['band'=16,'slab'=2] {'band'}, dimensions={1}, use_global_device_ids=true | all-gather | bytes 557056 | tf_op jit(solution)/shard_map/all_gather | solution.py:43
  52.8 0.8 bitcast_convert_fusion
  53.6 0.7 compare_select_fusion
  54.2 0.7 compare_and_fusion
  55.0 0.1 copy.16
  55.1 0.1 reshape.130
  55.1 6.2 %gather_fusion = bf16[2048,128]{1,0:T(8,128)(2,1)S(1)} fusion(bf16[2048,128]{1,0:T(8,128)(2,1)S(1)} %bitcast.61, s32[2048]{0:T(1024)S(1)} %broadcast_clamp_fusion), kind=kCustom, calls=%fused_computation | custom fusion | bytes 1056768 | tf_op jit(solution)/shard_map/while/body/eval_jaxpr/jit(_take)/gather | solution.py:24
  61.4 1.1 tanh_reduce_fusion
  62.5 0.7 multiply_convert_fusion.2
  63.1 0.0 all-gather.3.cloned.1.call-update
  63.2 0.0 all-reduce.6.cloned.1.call-start
  63.3 56.6 %all-gather.3.cloned.1.call-done = bf16[2048,512]{1,0:T(8,128)(2,1)} async-done(((bf16[128,512]{1,0:T(8,128)(2,1)}), bf16[2048,512]{1,0:T(8,128)(2,1)}) %all-gather.3.cloned.1.call-update) | async-done | bytes 2097168 | tf_op jit(solution)/shard_map/all_gather | solution.py:45
  119.9 1.7 dynamic-slice_select_fusion
  121.6 0.0 all-reduce.6.cloned.1.call-update
  121.6 0.0 all-reduce.8.cloned.1.call-start
  121.8 0.1 broadcast_in_dim.99
  122.0 0.1 copy.30
  122.1 0.6 dynamic-slice.3
  122.7 17.0 %all-reduce.6.cloned.1.call-done = bf16[256,512]{1,0:T(8,128)(2,1)} async-done(((bf16[256,512]{1,0:T(8,128)(2,1)}), bf16[256,512]{1,0:T(8,128)(2,1)}) %all-reduce.6.cloned.1.call-update) | async-done | bytes 262160 | tf_op jit(solution)/shard_map/psum | solution.py:13
  139.7 2.2 fusion.2
  142.0 0.1 copy.31
  142.1 1.2 fusion.13
  143.4 0.0 all-reduce.8.cloned.1.call-update
  143.4 0.0 all-reduce.10.cloned.1.call-start
  143.6 0.1 broadcast_in_dim.107
  143.7 19.0 %all-reduce.8.cloned.1.call-done = bf16[256,256]{0,1:T(8,128)(2,1)} async-done(((bf16[256,256]{0,1:T(8,128)(2,1)}), bf16[256,256]{0,1:T(8,128)(2,1)}) %all-reduce.8.cloned.1.call-update) | async-done | bytes 131088 | tf_op jit(solution)/shard_map/psum | solution.py:13
  162.7 0.9 convert_select_fusion
  163.6 0.1 copy.20
  163.7 1.0 fusion.8
  164.7 11.7 %cholesky.49 = f32[128,128]{1,0:T(8,128)S(1)} custom-call(f32[128,128]{1,0:T(8,128)S(1)} %cholesky.115), custom_call_target="Cholesky" | custom-call | tf_op jit(solution)/shard_map/jit(cholesky)/cholesky | solution.py:62
  176.5 9.8 %custom-call.14 = f32[1,128,128]{1,2,0:T(8,128)S(1)} custom-call(f32[1,128,128]{2,1,0:T(8,128)S(1)} %get-tuple-element.53), custom_call_target="InvertDiagBlocksLowerTriangular" | custom-call | tf_op jit(solution)/shard_map/jit(cholesky)/cholesky | solution.py:62
  186.3 0.2 fusion.17
  186.5 0.3 convolution_subtract_fusion.2
  186.8 11.7 %cholesky.103 = f32[128,128]{1,0:T(8,128)S(1)} custom-call(f32[128,128]{1,0:T(8,128)S(1)} %convolution_subtract_fusion.2), custom_call_target="Cholesky" | custom-call | tf_op jit(solution)/shard_map/jit(cholesky)/cholesky | solution.py:62
  198.5 0.1 copy.23
  198.6 0.1 copy.22
  198.7 0.1 copy.21
  198.8 0.7 compare_reduce_fusion
  201.0 0.1 triangular_solve.53
  201.1 4.5 %while.1 = (s32[]{:T(128)}, f32[256,256]{0,1:T(8,128)S(1)}, s32[2,2]{1,0:T(2,128)S(1)}, f32[2,128,128]{2,1,0:T(8,128)S(1)}, s32[]{:T(128)}) while((s32[]{:T(128)}, f32[256,256]{0,1:T(8,128)S(1)}, s32[2,2]{1,0:T(2,128)S(1)}, f32[2,128,128]{2,1,0:T(8,128)S(1)}, s32[]{:T(128)}) %tuple.33), condition=%wide.while_cond, body=%wide.while_body.sunk | while | flops 2 | bytes 393321 | solution.py:63
  201.2 0.6 fusion.33
  201.8 1.4 dynamic-slice.8
  203.2 0.1 copy.37
  203.4 0.6 fusion.33
  204.0 1.4 dynamic-slice.8
  205.4 0.1 copy.37
  205.5 20.3 %custom-call.15 = f32[2,128,128]{1,2,0:T(8,128)} custom-call(f32[2,128,128]{2,1,0:T(8,128)S(1)} %get-tuple-element.27), custom_call_target="InvertDiagBlocksLowerTriangular" | custom-call | tf_op jit(solution)/shard_map/triangular_solve | solution.py:63
  225.8 1.9 fusion.4
  227.8 3.6 convolution_subtract_fusion.1
  231.4 1.0 copy.25
  232.4 2.2 fusion.15
  234.6 2.2 fusion.3
  236.7 0.0 all-reduce.10.cloned.1.call-update
  236.8 0.0 all-reduce.12.cloned.1.call-start
  236.8 113.0 %all-reduce.10.cloned.1.call-done = bf16[2048,256]{1,0:T(8,128)(2,1)} async-done(((bf16[2048,256]{1,0:T(8,128)(2,1)}), bf16[2048,256]{1,0:T(8,128)(2,1)}) %all-reduce.10.cloned.1.call-update) | async-done | bytes 1048592 | tf_op jit(solution)/shard_map/psum | solution.py:13
  349.9 1.7 dynamic-slice_select_fusion.1
  351.5 0.0 all-reduce.12.cloned.1.call-update
  351.6 2.4 gather_fusion.1
  353.9 0.6 log_reduce_fusion
  355.2 40.4 %psum.39 = f32[]{:T(128)} all-reduce(f32[]{:T(128)S(6)} %select_n.147), channel_id=1, replica_groups=mesh['band'=16,'slab'=2] {'band'}, use_global_device_ids=true, to_apply=%region_10.11 | all-reduce | flops 1 | bytes 8 | tf_op jit(solution)/shard_map/psum | solution.py:74
  396.3 0.0 all-reduce.12.cloned.1.call-done
  396.3 1.4 fusion
  397.7 10.0 %copy.27 = f32[1,2048,1,256]{3,2,1,0:T(1,128)} copy(f32[1,2048,1,256]{3,1,2,0:T(8,128)S(1)} %fusion) | data formatting | bytes 4194304
  (31 shorter events, 0.4 us)
Async XLA Ops:
  7.2 54.2 %copy-start = (bf16[128,512]{1,0:T(8,128)(2,1)S(1)}, bf16[128,512]{1,0:T(8,128)(2,1)}, u32[]{:S(2)}) copy-start(bf16[128,512]{1,0:T(8,128)(2,1)} %param.7) | copy-start | bytes 393220
  7.2 112.7 %all-gather.3.cloned.1.call-start = ((), (), s32[]{:S(2)}) async-start(), calls=%async_computation | async-start | bytes 2228224 | tf_op jit(solution)/shard_map/all_gather | solution.py:45
  61.3 60.3 %copy-start.4 = (s32[16]{0:T(128)S(1)}, s32[16]{0:T(128)}, u32[]{:S(2)}) copy-start(s32[16]{0:T(128)} %param.9) | copy-start | bytes 196
  61.4 60.6 %copy-start.3 = (f32[256]{0:T(256)S(1)}, f32[256]{0:T(256)}, u32[]{:S(2)}) copy-start(f32[256]{0:T(256)} %param.8) | copy-start | bytes 3076
  63.2 76.6 %all-reduce.6.cloned.1.call-start = ((), (), s32[]{:S(2)}) async-start(), calls=%async_computation.1 | async-start | bytes 524288 | tf_op jit(solution)/shard_map/psum | solution.py:13
  121.6 41.0 %all-reduce.8.cloned.1.call-start = ((), (), s32[]{:S(2)}) async-start(), calls=%async_computation.2 | async-start | bytes 262144 | tf_op jit(solution)/shard_map/psum | solution.py:13
  143.4 206.4 %all-reduce.10.cloned.1.call-start = ((), (), s32[]{:S(2)}) async-start(), calls=%async_computation.3 | async-start | bytes 2097152 | tf_op jit(solution)/shard_map/psum | solution.py:13
  205.5 20.3 %copy-start.1 = (f32[256,256]{0,1:T(8,128)}, f32[256,256]{0,1:T(8,128)S(1)}, u32[]{:S(2)}) copy-start(f32[256,256]{0,1:T(8,128)S(1)} %get-tuple-element.110) | copy-start | bytes 786436
  236.8 159.5 %all-reduce.12.cloned.1.call-start = ((), (), s32[]{:S(2)}) async-start(), calls=%async_computation.4 | async-start | bytes 262144 | tf_op jit(solution)/shard_map/psum | solution.py:13
  349.9 46.5 %copy-start.2 = (bf16[2048,256]{1,0:T(8,128)(2,1)S(1)}, bf16[2048,256]{1,0:T(8,128)(2,1)}, u32[]{:S(2)}) copy-start(bf16[2048,256]{1,0:T(8,128)(2,1)} %all-reduce.10.cloned.1.call-done) | copy-start | bytes 3145732
Sparse Core Ops, SparseCore 0:
  63.3 56.5 all-gather.2
  122.8 16.8 all-reduce.5
  143.5 19.0 all-reduce.7
  236.9 112.9 all-reduce.9
  352.7 16.9 all-reduce.11
where the time goes:
time: 416 us; the launch traced here: 415 us
  waiting for transfers between devices  206 us (50%)
  blocking collectives  86 us (21%)
  other arithmetic  66.6 us (16%)
  local copies, waits for them, and re-layouts  25.5 us (6%)
  between operations  18.1 us (4%)
  matrix products  12.9 us (3%)
    psum x4, waiting for transfers between devices, from_root(): return lax.psum(block, axis)  149 us
    all_gather x1, waiting for transfers between devices, on_device(): slab_factor = lax.all_gather(own_factor, 'band', axis=0, tiled=True)  56.6 us
    all_gather x1, blocking collectives, on_device(): slab_feats = lax.all_gather(own_feats, 'band', axis=0, tiled=True)  45.6 us
    psum x1, blocking collectives, on_device(): total = lax.psum(term, 'band')  40.4 us
    another operation x6, other arithmetic, on_device(): lower = jnp.linalg.cholesky(pivot_block)  34 us
    another operation x3, other arithmetic, on_device(): lax.linalg.triangular_solve(lower, matrix.reshape(count, block), left_sid...  20.3 us
    unnamed x13, local copies, waits for them, and re-layouts  10.3 us
  transfers between devices with their start and end apart: 5, of which 4 were waited for; matrix products, arithmetic and copies ran while one was open for 1% of the time, Pallas kernels for 0%

commit v1 on v0

v1 whole, which is shorter than its diff:
```python
import functools
import math

import jax
import jax.numpy as jnp
from jax import lax
from jax.experimental import pallas as pl
from jax.experimental.pallas import tpu as pltpu
from jax.sharding import PartitionSpec as P

STEPS = 1
MESH = pl.DeviceIdType.MESH
TAIL = 16
HI = lax.Precision.HIGHEST


def slots(buf, origin, rows, piece):
    start, size = piece
    return buf.at[pl.ds(pl.multiple_of(origin * rows + start, 16), size), :]


def tree_gather(n, me, buf, rows, pieces, send_sem, recv_sem):
    depth = n // 4
    z, y, x = me // 4, (me // 2) % 2, me % 2
    xn = me + 1 - 2 * x
    yn = me + 2 - 4 * y
    xyn = xn + 2 - 4 * y
    targets = (me + 4, me - 4, xn, yn)
    sent = []

    def copy(origin, piece, way):
        block = slots(buf, origin, rows, pieces[piece])
        return pltpu.make_async_remote_copy(
            src_ref=block,
            dst_ref=block,
            send_sem=send_sem.at[(origin * 2 + piece) * 4 + way],
            recv_sem=recv_sem.at[origin * 2 + piece],
            device_id={"band": targets[way]},
            device_id_type=MESH,
        )

    def send(origin, piece, way, cond):
        sent.append((origin, piece, way, cond))
        if cond is None:
            copy(origin, piece, way).start()
        else:
            pl.when(cond)(lambda: copy(origin, piece, way).start())

    def arrived(origin, piece, cond):
        if cond is None:
            copy(origin, piece, 2).wait_recv()
        else:
            pl.when(cond)(lambda: copy(origin, piece, 2).wait_recv())

    def both(a, b):
        return b if a is None else jnp.logical_and(a, b)

    def exists(dz):
        if dz == 0:
            return None
        return z < depth - dz if dz > 0 else z >= -dz

    def line(dz):
        cond = exists(dz)
        origin = me + 4 * dz
        for piece in (0, 1):
            if dz:
                arrived(origin, piece, cond)
            if dz <= 0:
                send(origin, piece, 0, both(cond, z < depth - 1))
            if dz >= 0:
                send(origin, piece, 1, both(cond, z > 0))
            for way in (2 + piece, 3 - piece):
                send(origin, piece, way, cond)

    def side(dz):
        cond = exists(dz)
        arrived(xn + 4 * dz, 0, cond)
        send(xn + 4 * dz, 0, 3, cond)
        arrived(yn + 4 * dz, 1, cond)
        send(yn + 4 * dz, 1, 2, cond)

    line(0)
    for far in range(1, depth + 1):
        if far < depth:
            line(far)
            line(-far)
        side(far - 1)
        if far > 1:
            side(1 - far)
    for dz in range(1 - depth, depth):
        cond = exists(dz)
        arrived(yn + 4 * dz, 0, cond)
        arrived(xyn + 4 * dz, 0, cond)
        arrived(xn + 4 * dz, 1, cond)
        arrived(xyn + 4 * dz, 1, cond)

    def drain():
        for origin, piece, way, cond in sent:
            if cond is None:
                copy(origin, piece, way).wait_send()
            else:
                pl.when(cond)(functools.partial(lambda o, p, w: copy(o, p, w).wait_send(), origin, piece, way))

    return drain


def direct_gather(n, me, buf, rows, pieces, send_sem, recv_sem):
    whole = (0, sum(size for _, size in pieces))

    def copy(origin, shift):
        block = slots(buf, origin, rows, whole)
        return pltpu.make_async_remote_copy(
            src_ref=block,
            dst_ref=block,
            send_sem=send_sem.at[shift],
            recv_sem=recv_sem.at[shift],
            device_id={"band": lax.rem(me + shift, n)},
            device_id_type=MESH,
        )

    @pl.loop(1, n)
    def _(shift):
        copy(me, shift).start()

    @pl.loop(1, n)
    def _(shift):
        copy(lax.rem(me + n - shift, n), shift).wait_recv()

    def drain():
        @pl.loop(1, n)
        def _(shift):
            copy(me, shift).wait_send()

    return drain


def assemble_kernel(
    n, groups, block, scale,
    order_ref, nbrs_ref, feats_ref, w_ref, stiff_ref,
    slab_ref, column_ref, pivot_ref, pstiff_ref,
    gathered, wide, near, pivots,
    fsend, frecv, ssend, srecv, csend, crecv, psend, precv,
):
    me = lax.axis_index("band")
    slab = lax.axis_index("slab")
    beads = feats_ref.shape[0]
    links = nbrs_ref.shape[0] // beads
    frows = beads + TAIL
    tree = n == 16
    gather = tree_gather if tree else direct_gather
    home = me // groups
    owner = lax.rem(me, groups)

    barrier = pltpu.get_barrier_semaphore()
    if tree:
        z, y, x = me // 4, (me // 2) % 2, me % 2
        mates = [(me + 1 - 2 * x, None), (me + 2 - 4 * y, None), (me + 4, z < n // 4 - 1), (me - 4, z > 0)]
        for mate, cond in mates:
            def greet(mate=mate):
                pl.semaphore_signal(barrier, inc=1, device_id={"band": mate}, device_id_type=MESH)
            greet() if cond is None else pl.when(cond)(greet)
    else:
        @pl.loop(1, n)
        def _(shift):
            pl.semaphore_signal(barrier, inc=1, device_id={"band": lax.rem(me + shift, n)}, device_id_type=MESH)
    for shift in range(1, groups):
        pl.semaphore_signal(barrier, inc=1, device_id={"slab": lax.rem(slab + shift, groups)}, device_id_type=MESH)

    mine = pl.multiple_of(me * frows, 16)
    gathered[pl.ds(mine, beads), :] = feats_ref[...]
    stiff = stiff_ref[...]
    high = stiff.astype(jnp.bfloat16).astype(jnp.float32)
    mid = (stiff - high).astype(jnp.bfloat16).astype(jnp.float32)
    low = stiff - high - mid
    parts = jnp.concatenate([high, mid, low], axis=0)
    tail = jnp.concatenate([parts, jnp.zeros((TAIL - parts.shape[0], parts.shape[1]), jnp.float32)], axis=0)
    gathered[pl.ds(mine + beads, TAIL), :] = tail.astype(jnp.bfloat16)

    if tree:
        inner = jnp.logical_and(z > 0, z < n // 4 - 1)
        pl.semaphore_wait(barrier, jnp.where(inner, groups + 3, groups + 2))
    else:
        pl.semaphore_wait(barrier, n - 1 + groups - 1)

    half = beads // 2
    drain_feats = gather(n, me, gathered, frows, ((0, half), (half, half + TAIL)), fsend, frecv)
    for origin in range(n):
        wide[pl.ds(origin * beads, beads), :] = gathered[pl.ds(origin * frows, beads), :].astype(jnp.float32)

    chunk = 16
    first = pl.multiple_of(me * beads, 16)

    @pl.loop(0, beads // chunk)
    def _(step):
        base = pl.multiple_of(step * chunk, chunk)
        for link in range(links):
            for bead in range(chunk):
                row = nbrs_ref[link * beads + base + bead]
                near[pl.ds(link * chunk + bead, 1), :] = wide[pl.ds(row, 1), :]
        own = feats_ref[pl.ds(base, chunk), :].astype(jnp.float32)
        mixed = near[...].reshape(links, chunk, -1) * own[None]
        mixed = mixed.reshape(links * chunk, -1).astype(jnp.bfloat16)
        pre = jnp.dot(mixed, w_ref[...], preferred_element_type=jnp.float32)
        total = jnp.sum(jnp.tanh(pre).reshape(links, chunk, -1), axis=0)
        slab_ref[pl.ds(first + base, chunk), :] = (total * scale).astype(jnp.bfloat16)

    drain_slab = gather(n, me, slab_ref, beads, ((0, half), (half, half)), ssend, srecv)

    chosen = order_ref[:, 0:1]
    blocks = slab_ref.shape[0] // block
    passed = [(chosen >= (r + 1) * groups).astype(jnp.int32) for r in range(blocks)]
    number = sum(passed)
    lane = chosen - number * groups

    def mask(flag, lanes):
        return jnp.broadcast_to(flag.astype(jnp.float32), (16, lanes)).astype(jnp.bfloat16)

    channels = slab_ref.shape[1]
    masks = [mask(number == r, channels) for r in range(blocks)]
    for row in range(0, block, 16):
        picked = sum(slab_ref[r * block + row:r * block + row + 16, :] * masks[r] for r in range(blocks))
        pivots[pl.ds(pl.multiple_of(slab * block + row, 16), 16), :] = picked

    def pivot_copy(shift, source):
        part = pivots.at[pl.ds(pl.multiple_of(source * block, 16), block), :]
        return pltpu.make_async_remote_copy(
            src_ref=part, dst_ref=part, send_sem=psend.at[shift], recv_sem=precv.at[shift],
            device_id={"slab": lax.rem(slab + shift, groups)}, device_id_type=MESH,
        )

    for shift in range(1, groups):
        pivot_copy(shift, slab).start()

    def column_copy(shift):
        return pltpu.make_async_remote_copy(
            src_ref=column_ref, dst_ref=column_ref, send_sem=csend.at[shift], recv_sem=crecv,
            device_id={"slab": lax.rem(slab + shift, groups)}, device_id_type=MESH,
        )

    @pl.when(slab == owner)
    def _():
        column_ref[...] = slab_ref[pl.ds(pl.multiple_of(home * block, 16), block), :]
        for shift in range(1, groups):
            column_copy(shift).start()
        for shift in range(1, groups):
            column_copy(shift).wait_send()

    @pl.when(slab != owner)
    def _():
        column_copy(1).wait_recv()

    for shift in range(1, groups):
        pivot_copy(shift, lax.rem(slab + groups - shift, groups)).wait_recv()
    masks = [mask(lane == g, channels) for g in range(groups)]
    for row in range(0, block, 16):
        pivot_ref[row:row + 16, :] = sum(
            pivots[g * block + row:g * block + row + 16, :] * masks[g] for g in range(groups)
        )
    held = sum(
        gathered[b * frows + beads:(b + 1) * frows, :].astype(jnp.float32)
        * jnp.broadcast_to((chosen == b).astype(jnp.float32), (TAIL, gathered.shape[1]))
        for b in range(n)
    )
    lanes = block // held.shape[1]
    pstiff_ref[...] = held[0:lanes] + held[lanes:2 * lanes] + held[2 * lanes:3 * lanes]

    for shift in range(1, groups):
        pivot_copy(shift, slab).wait_send()
    drain_feats()
    drain_slab()


def as_row(pieces):
    return jnp.concatenate([pieces[i:i + 1, :] for i in range(pieces.shape[0])], axis=1)


def eliminate(fp_ref, pstiff_ref, work, whitened, log_ref):
    block, width = fp_ref.shape
    step = 32
    fp = fp_ref[...]
    square = lax.dot_general(fp, fp, (((1,), (1,)), ((), ())), preferred_element_type=jnp.float32)
    rows = lax.broadcasted_iota(jnp.int32, (block, block), 0)
    cols = lax.broadcasted_iota(jnp.int32, (block, block), 1)
    work[:, :block] = square + jnp.where(rows == cols, as_row(pstiff_ref[...]), 0.0)
    work[:, block:] = fp.astype(jnp.float32)
    down = lax.broadcasted_iota(jnp.int32, (step, 1), 0)
    eye = (
        lax.broadcasted_iota(jnp.int32, (step, step), 0) == lax.broadcasted_iota(jnp.int32, (step, step), 1)
    ).astype(jnp.float32)
    logs = jnp.zeros((1, 1), jnp.float32)
    for start in range(0, block, step):
        both = jnp.concatenate([work[start:start + step, start:start + step], eye], axis=1)
        for j in range(step - 1):
            lead = both[j:j + 1, :]
            ratio = both[:, j:j + 1] * (1.0 / lead[:, j:j + 1])
            both = both - jnp.where(down > j, ratio, 0.0) * lead
        diag = jnp.sum(both[:, :step] * eye, axis=1, keepdims=True)
        logs = logs + jnp.sum(jnp.log(diag), axis=0, keepdims=True)
        inverse = both[:, step:] * lax.rsqrt(diag)
        done = jnp.dot(inverse, work[start:start + step, :], precision=HI, preferred_element_type=jnp.float32)
        whitened[start:start + step, :] = done[:, block:]
        after = start + step
        if after < block:
            low = after // 128 * 128
            work[low:, low:] = work[low:, low:] - lax.dot_general(
                done[:, low:block], done[:, low:], (((0,), (0,)), ((), ())),
                precision=HI, preferred_element_type=jnp.float32,
            )
    log_ref[...] = jnp.broadcast_to(logs * (1.0 / (STEPS * block)), log_ref.shape)


def finish_kernel(
    groups, order_ref, slab_ref, column_ref, fp_ref, pstiff_ref, stiff_ref,
    out_ref, log_ref, work, whitened, whigh, wlow, pcol,
):
    me = lax.axis_index("band")
    slab = lax.axis_index("slab")
    r = pl.program_id(0)
    pivot = order_ref[0]
    block = fp_ref.shape[0]
    nt = (((1,), (1,)), ((), ()))

    def panel(rows):
        return lax.dot_general(rows, whigh[...], nt, preferred_element_type=jnp.float32) + lax.dot_general(
            rows, wlow[...], nt, preferred_element_type=jnp.float32
        )

    @pl.when(r == 0)
    def _():
        eliminate(fp_ref, pstiff_ref, work, whitened, log_ref)
        w = whitened[...]
        high = w.astype(jnp.bfloat16)
        whigh[...] = high
        wlow[...] = (w - high.astype(jnp.float32)).astype(jnp.bfloat16)
        pcol[...] = jnp.where(me == pivot, 0.0, panel(column_ref[...])).astype(jnp.bfloat16)

    here = r * groups + slab
    rows = slab_ref[...]
    own = jnp.where(here == pivot, 0.0, panel(rows)).astype(jnp.bfloat16)
    value = lax.dot_general(rows, column_ref[...], nt, preferred_element_type=jnp.float32)
    value = value - lax.dot_general(own, pcol[...], nt, preferred_element_type=jnp.float32)
    iota = [lax.broadcasted_iota(jnp.int32, value.shape, d) for d in (0, 1)]
    on = jnp.logical_and(iota[0] == iota[1], here == me)
    value = value + jnp.where(on, as_row(stiff_ref[...]), 0.0)
    parts = block // 128
    for part in range(parts):
        out_ref[pl.ds(part, block, stride=parts), :] = value[:, part * 128:(part + 1) * 128]


def on_device(n, groups, feats, nbrs, w_pair, stiff, order):
    own_feats = feats[0]
    beads, width = own_feats.shape
    links = nbrs.shape[2]
    channels = w_pair.shape[1]
    block = stiff.shape[0]
    count = n * beads
    flat = nbrs[0].T.reshape(links * beads)
    stiff2 = stiff.reshape(block // 128, 128)
    scale = 1.5 / math.sqrt(links * channels)
    vmem = pl.BlockSpec(memory_space=pltpu.VMEM)
    smem = pl.BlockSpec(memory_space=pltpu.SMEM)
    dma = pltpu.SemaphoreType.DMA
    slab_factor, column, pivot_factor, pivot_stiff = pl.pallas_call(
        functools.partial(assemble_kernel, n, groups, block, scale),
        out_shape=(
            jax.ShapeDtypeStruct((count, channels), jnp.bfloat16),
            jax.ShapeDtypeStruct((block, channels), jnp.bfloat16),
            jax.ShapeDtypeStruct((block, channels), jnp.bfloat16),
            jax.ShapeDtypeStruct((block // 128, 128), jnp.float32),
        ),
        in_specs=[vmem, smem, vmem, vmem, vmem],
        out_specs=(vmem, vmem, vmem, vmem),
        scratch_shapes=[
            pltpu.VMEM((n * (beads + TAIL), width), jnp.bfloat16),
            pltpu.VMEM((count, width), jnp.float32),
            pltpu.VMEM((links * 16, width), jnp.float32),
            pltpu.VMEM((groups * block, channels), jnp.bfloat16),
            dma((n * 8,)), dma((n * 2,)), dma((n * 8,)), dma((n * 2,)),
            dma((groups,)), dma(()), dma((groups,)), dma((groups,)),
        ],
        compiler_params=pltpu.CompilerParams(
            collective_id=0, has_side_effects=True, vmem_limit_bytes=32 * 1024 * 1024
        ),
        name="assemble",
    )(order.reshape(1, -1), flat, own_feats, w_pair, stiff2)

    whole = lambda shape: pl.BlockSpec(shape, lambda r: (0,) * len(shape))
    out, logs = pl.pallas_call(
        functools.partial(finish_kernel, groups),
        grid=(count // block,),
        out_shape=(
            jax.ShapeDtypeStruct((count * block // 128, 128), jnp.float32),
            jax.ShapeDtypeStruct((8, 128), jnp.float32),
        ),
        in_specs=[
            smem,
            pl.BlockSpec((block, channels), lambda r: (r, 0)),
            whole((block, channels)), whole((block, channels)),
            whole((block // 128, 128)), whole((block // 128, 128)),
        ],
        out_specs=(
            pl.BlockSpec((block * block // 128, 128), lambda r: (r, 0)),
            whole((8, 128)),
        ),
        scratch_shapes=[
            pltpu.VMEM((block, block + channels), jnp.float32),
            pltpu.VMEM((block, channels), jnp.float32),
            pltpu.VMEM((block, channels), jnp.bfloat16),
            pltpu.VMEM((block, channels), jnp.bfloat16),
            pltpu.VMEM((block, block), jnp.bfloat16),
        ],
        compiler_params=pltpu.CompilerParams(vmem_limit_bytes=32 * 1024 * 1024),
        name="finish",
    )(order, slab_factor, column, pivot_factor, pivot_stiff, stiff2)
    return out.reshape(1, count, 1, block), logs[0, 0]


def solution(mesh):
    in_specs = (P("slab", "band", None), P("slab", "band", None), P(), P("band"), P())
    out_specs = (P("slab", None, "band", None), P())
    return jax.shard_map(
        functools.partial(on_device, mesh.shape["band"], mesh.shape["slab"]),
        mesh=mesh, in_specs=in_specs, out_specs=out_specs, check_vma=False,
    )
```

time: 416 us -> 83.4 us (0.20)
  waiting for transfers between devices: 206 us -> 0 us
  blocking collectives: 86 us -> 0 us
  Pallas kernels: 0 us -> 78.3 us
  other arithmetic: 66.6 us -> 0 us
  local copies, waits for them, and re-layouts: 25.5 us -> 4.2 us
  between operations: 18.1 us -> 0.65 us
  matrix products: 12.9 us -> 0 us
    psum x4 -> x0, waiting for transfers between devices: 149 us -> none  [from_root(): return lax.psum(block, axis)]
    pallas_call x0 -> x2, Pallas kernels: none -> 78.3 us  [the longest x1 44.8 us: on_device(): pl.pallas_call(functools.partial(assemble_kernel, n, groups, block, scale...]
    all_gather x1 -> x0, waiting for transfers between devices: 56.6 us -> none  [on_device(): slab_factor = lax.all_gather(own_factor, 'band', axis=0, tiled=True)]
    another operation x9 -> x0, other arithmetic: 54.4 us -> none  [the longest x6 34 us: on_device(): lower = jnp.linalg.cholesky(pivot_block)]
    all_gather x1 -> x0, blocking collectives: 45.6 us -> none  [on_device(): slab_feats = lax.all_gather(own_feats, 'band', axis=0, tiled=True)]
    psum x1 -> x0, blocking collectives: 40.4 us -> none  [on_device(): total = lax.psum(term, 'band')]
    gather x2 -> x0, local copies, waits for them, and re-layouts: 8.55 us -> none  [the longest x1 6.18 us: one_block(): near = jnp.take(slab_feats, links, axis=0)]
    select_n x7 -> x0, other arithmetic: 8.45 us -> none  [the longest x4 6.8 us: from_root(): jnp.where(lax.axis_index(axis) == owner, block, jnp.zeros_like(block))]
  transfers between devices with their start and end apart: 5 -> 0, of which waited for: 4 -> 0; matrix products, arithmetic and copies ran while one was open for 1% -> 0% of each run, Pallas kernels for 0% -> 0%
where the time goes in v1:
time: 83.4 us; the launch traced here: 83.1 us
  Pallas kernels  78.3 us (94%)
  local copies, waits for them, and re-layouts  4.2 us (5%)
    pallas_call x1, Pallas kernels, on_device(): pl.pallas_call(functools.partial(assemble_kernel, n, groups, block, scale...  44.8 us
    pallas_call x1, Pallas kernels, on_device(): pl.pallas_call(functools.partial(finish_kernel, groups), grid=(count // b...  33.4 us
    unnamed x10, local copies, waits for them, and re-layouts  3.68 us

profile of v1, /device:TPU:0, one launch (start us, length us, event | category | flops | bytes accessed | tf_op | source)
XLA Modules:
  0.0 83.1 jit_solution(11571698854392703729)
XLA Ops:
  0.6 0.0 copy-start
  0.6 0.9 %copy-done = bf16[128,512]{1,0:T(8,128)(2,1)S(1)} copy-done((bf16[128,512]{1,0:T(8,128)(2,1)S(1)}, bf16[128,512]{1,0:T(8,128)(2,1)}, u32[]{:S(2)}) %copy-start) | copy-done | bytes 131096
  1.5 0.0 copy-start.1
  1.5 0.8 copy-done.1
  2.3 0.0 copy-start.2
  2.3 0.7 copy-done.2
  3.0 0.0 copy-start.3
  3.0 0.7 copy-done.3
  3.7 0.0 copy-start.4
  3.7 0.7 copy-done.4
  4.3 44.8 %assemble.1 = (bf16[2048,512]{1,0:T(8,128)(2,1)S(1)}, bf16[256,512]{1,0:T(8,128)(2,1)S(1)}, bf16[256,512]{1,0:T(8,128)(2,1)S(1)}, f32[2,128]{1,0:T(2,128)S(1)}) custom-call(s32[1,16]{1,0:T(1,128)S(1)} %bitcast.14, s32[2048]{0:T(1024)S(1)} %bitcast.11, bf16[128,128]{1,0:T(8,128)(2,1)S(1)} %bitcast.10, bf16[128,512]{1,0:T(8,128)(2,1)S(1)} %copy-done, ...), custom_call_target="tpu_custom_call" | custom-call | tf_op jit(solution)/shard_map/assemble/pallas_call | solution.py:364
  49.2 33.4 %finish.1 = (f32[4096,128]{1,0:T(8,128)}, f32[8,128]{1,0:T(8,128)S(1)}) custom-call(s32[16]{0:T(128)S(1)} %copy-done.4, bf16[2048,512]{1,0:T(8,128)(2,1)S(1)} %get-tuple-element.8.slab_ref, bf16[256,512]{1,0:T(8,128)(2,1)S(1)} %get-tuple-element.9.column_ref, bf16[256,512]{1,0:T(8,128)(2,1)S(1)} %get-tuple-element.10.fp_ref, ...), custom_call_target="tpu_custom_call" | custom-call | tf_op jit(solution)/shard_map/finish/pallas_call | solution.py:389
  82.6 0.5 slice.3
Async XLA Ops:
  0.6 0.9 %copy-start = (bf16[128,512]{1,0:T(8,128)(2,1)S(1)}, bf16[128,512]{1,0:T(8,128)(2,1)}, u32[]{:S(2)}) copy-start(bf16[128,512]{1,0:T(8,128)(2,1)} %w_ref.1) | copy-start | bytes 393220
  1.5 0.8 copy-start.1
  2.3 0.7 copy-start.2
  3.0 0.7 copy-start.3
  3.7 0.7 copy-start.4

commit v2 on v1

--- a/solution.py
+++ b/solution.py
@@ -19,7 +19,7 @@
     return buf.at[pl.ds(pl.multiple_of(origin * rows + start, 16), size), :]
 
 
-def tree_gather(n, me, buf, rows, pieces, send_sem, recv_sem):
+def tree_gather(n, me, buf, rows, pieces, send_sem, recv_sem, make=None):
     depth = n // 4
     z, y, x = me // 4, (me // 2) % 2, me % 2
     xn = me + 1 - 2 * x
@@ -66,6 +66,8 @@
         for piece in (0, 1):
             if dz:
                 arrived(origin, piece, cond)
+            elif make is not None:
+                make(piece)
             if dz <= 0:
                 send(origin, piece, 0, both(cond, z < depth - 1))
             if dz >= 0:
@@ -105,7 +107,7 @@
     return drain
 
 
-def direct_gather(n, me, buf, rows, pieces, send_sem, recv_sem):
+def direct_gather(n, me, buf, rows, pieces, send_sem, recv_sem, make=None):
     whole = (0, sum(size for _, size in pieces))
 
     def copy(origin, shift):
@@ -118,6 +120,10 @@
             device_id={"band": lax.rem(me + shift, n)},
             device_id_type=MESH,
         )
+
+    if make is not None:
+        make(0)
+        make(1)
 
     @pl.loop(1, n)
     def _(shift):
@@ -191,21 +197,22 @@
     chunk = 16
     first = pl.multiple_of(me * beads, 16)
 
-    @pl.loop(0, beads // chunk)
-    def _(step):
-        base = pl.multiple_of(step * chunk, chunk)
-        for link in range(links):
-            for bead in range(chunk):
-                row = nbrs_ref[link * beads + base + bead]
-                near[pl.ds(link * chunk + bead, 1), :] = wide[pl.ds(row, 1), :]
-        own = feats_ref[pl.ds(base, chunk), :].astype(jnp.float32)
-        mixed = near[...].reshape(links, chunk, -1) * own[None]
-        mixed = mixed.reshape(links * chunk, -1).astype(jnp.bfloat16)
-        pre = jnp.dot(mixed, w_ref[...], preferred_element_type=jnp.float32)
-        total = jnp.sum(jnp.tanh(pre).reshape(links, chunk, -1), axis=0)
-        slab_ref[pl.ds(first + base, chunk), :] = (total * scale).astype(jnp.bfloat16)
-
-    drain_slab = gather(n, me, slab_ref, beads, ((0, half), (half, half)), ssend, srecv)
+    def make(piece):
+        @pl.loop(piece * half // chunk, (piece + 1) * half // chunk)
+        def _(step):
+            base = pl.multiple_of(step * chunk, chunk)
+            for link in range(links):
+                for bead in range(chunk):
+                    row = nbrs_ref[link * beads + base + bead]
+                    near[pl.ds(link * chunk + bead, 1), :] = wide[pl.ds(row, 1), :]
+            own = feats_ref[pl.ds(base, chunk), :].astype(jnp.float32)
+            mixed = near[...].reshape(links, chunk, -1) * own[None]
+            mixed = mixed.reshape(links * chunk, -1).astype(jnp.bfloat16)
+            pre = jnp.dot(mixed, w_ref[...], preferred_element_type=jnp.float32)
+            total = jnp.sum(jnp.tanh(pre).reshape(links, chunk, -1), axis=0)
+            slab_ref[pl.ds(first + base, chunk), :] = (total * scale).astype(jnp.bfloat16)
+
+    drain_slab = gather(n, me, slab_ref, beads, ((0, half), (half, half)), ssend, srecv, make)
 
     chosen = order_ref[:, 0:1]
     blocks = slab_ref.shape[0] // block
@@ -275,44 +282,73 @@
     return jnp.concatenate([pieces[i:i + 1, :] for i in range(pieces.shape[0])], axis=1)
 
 
-def eliminate(fp_ref, pstiff_ref, work, whitened, log_ref):
-    block, width = fp_ref.shape
+def split(value):
+    high = value.astype(jnp.bfloat16)
+    return high, (value - high.astype(jnp.float32)).astype(jnp.bfloat16)
+
+
+def dot3(left, right, dims):
+    lh, ll = split(left)
+    rh, rl = split(right)
+    dims = (dims, ((), ()))
+    mul = lambda a, b: lax.dot_general(a, b, dims, preferred_element_type=jnp.float32)
+    return mul(lh, rh) + (mul(lh, rl) + mul(ll, rh))
+
+
+def small_inverse(both):
+    size, lanes = both.shape
+    kept = []
+    for start in range(0, size, 8):
+        rows = both.shape[0]
+        down = lax.broadcasted_iota(jnp.int32, (rows, lanes), 0)
+        cols = [jnp.broadcast_to(both[:, start + m:start + m + 1], (rows, lanes)) for m in range(8)]
+        for k in range(8):
+            ratio = jnp.where(down > k, cols[k] * (1.0 / cols[k][k:k + 1, :]), 0.0)
+            for m in range(k + 1, 8):
+                cols[m] = cols[m] - ratio * cols[m][k:k + 1, :]
+            both = both - ratio * both[k:k + 1, :]
+        kept.append(both[:8])
+        both = both[8:]
+    return jnp.concatenate(kept, axis=0)
+
+
+def eliminate(fp_ref, pstiff_ref, work, ident, lowinv, log_ref):
+    block = fp_ref.shape[0]
     step = 32
     fp = fp_ref[...]
     square = lax.dot_general(fp, fp, (((1,), (1,)), ((), ())), preferred_element_type=jnp.float32)
     rows = lax.broadcasted_iota(jnp.int32, (block, block), 0)
     cols = lax.broadcasted_iota(jnp.int32, (block, block), 1)
-    work[:, :block] = square + jnp.where(rows == cols, as_row(pstiff_ref[...]), 0.0)
-    work[:, block:] = fp.astype(jnp.float32)
-    down = lax.broadcasted_iota(jnp.int32, (step, 1), 0)
+    work[...] = square + jnp.where(rows == cols, as_row(pstiff_ref[...]), 0.0)
+    ident[...] = (rows == cols).astype(jnp.float32)
+    lowinv[...] = jnp.zeros(lowinv.shape, jnp.float32)
     eye = (
         lax.broadcasted_iota(jnp.int32, (step, step), 0) == lax.broadcasted_iota(jnp.int32, (step, step), 1)
     ).astype(jnp.float32)
     logs = jnp.zeros((1, 1), jnp.float32)
     for start in range(0, block, step):
-        both = jnp.concatenate([work[start:start + step, start:start + step], eye], axis=1)
-        for j in range(step - 1):
-            lead = both[j:j + 1, :]
-            ratio = both[:, j:j + 1] * (1.0 / lead[:, j:j + 1])
-            both = both - jnp.where(down > j, ratio, 0.0) * lead
+        after = start + step
+        both = small_inverse(jnp.concatenate([work[start:after, start:after], eye], axis=1))
         diag = jnp.sum(both[:, :step] * eye, axis=1, keepdims=True)
         logs = logs + jnp.sum(jnp.log(diag), axis=0, keepdims=True)
         inverse = both[:, step:] * lax.rsqrt(diag)
-        done = jnp.dot(inverse, work[start:start + step, :], precision=HI, preferred_element_type=jnp.float32)
-        whitened[start:start + step, :] = done[:, block:]
-        after = start + step
-        if after < block:
-            low = after // 128 * 128
-            work[low:, low:] = work[low:, low:] - lax.dot_general(
-                done[:, low:block], done[:, low:], (((0,), (0,)), ((), ())),
-                precision=HI, preferred_element_type=jnp.float32,
-            )
+        low = after // 128 * 128
+        high = -(-after // 128) * 128
+        if after == block:
+            lowinv[start:after, :] = dot3(inverse, ident[start:after, :], ((1,), (0,)))
+            break
+        wide = jnp.concatenate([work[start:after, low:], ident[start:after, :high]], axis=1)
+        done = dot3(inverse, wide, ((1,), (0,)))
+        lowinv[start:after, :high] = done[:, block - low:]
+        change = dot3(done[:, :block - low], done, ((0,), (0,)))
+        work[low:, low:] = work[low:, low:] - change[:, :block - low]
+        ident[low:, :high] = ident[low:, :high] - change[:, block - low:]
     log_ref[...] = jnp.broadcast_to(logs * (1.0 / (STEPS * block)), log_ref.shape)
 
 
 def finish_kernel(
     groups, order_ref, slab_ref, column_ref, fp_ref, pstiff_ref, stiff_ref,
-    out_ref, log_ref, work, whitened, whigh, wlow, pcol,
+    out_ref, log_ref, work, ident, lowinv, whigh, wlow, pcol,
 ):
     me = lax.axis_index("band")
     slab = lax.axis_index("slab")
@@ -328,11 +364,13 @@
 
     @pl.when(r == 0)
     def _():
-        eliminate(fp_ref, pstiff_ref, work, whitened, log_ref)
-        w = whitened[...]
-        high = w.astype(jnp.bfloat16)
-        whigh[...] = high
-        wlow[...] = (w - high.astype(jnp.float32)).astype(jnp.bfloat16)
+        eliminate(fp_ref, pstiff_ref, work, ident, lowinv, log_ref)
+        ih, il = split(lowinv[...])
+        fp = fp_ref[...]
+        w = jnp.dot(ih, fp, preferred_element_type=jnp.float32) + jnp.dot(
+            il, fp, preferred_element_type=jnp.float32
+        )
+        whigh[...], wlow[...] = split(w)
         pcol[...] = jnp.where(me == pivot, 0.0, panel(column_ref[...])).astype(jnp.bfloat16)
 
     here = r * groups + slab
@@ -404,8 +442,9 @@
             whole((8, 128)),
         ),
         scratch_shapes=[
-            pltpu.VMEM((block, block + channels), jnp.float32),
-            pltpu.VMEM((block, channels), jnp.float32),
+            pltpu.VMEM((block, block), jnp.float32),
+            pltpu.VMEM((block, block), jnp.float32),
+            pltpu.VMEM((block, block), jnp.float32),
             pltpu.VMEM((block, channels), jnp.bfloat16),
             pltpu.VMEM((block, channels), jnp.bfloat16),
             pltpu.VMEM((block, block), jnp.bfloat16),

time: 83.4 us -> 67.8 us (0.81)
  Pallas kernels: 78.3 us -> 62.6 us
    pallas_call x1, Pallas kernels: 33.4 us -> 18.4 us  [on_device(): pl.pallas_call(functools.partial(finish_kernel, groups), grid=(count // b...]
where the time goes in v2:
time: 67.8 us; the launch traced here: 67.5 us
  Pallas kernels  62.6 us (92%)
  local copies, waits for them, and re-layouts  4.2 us (6%)
    pallas_call x1, Pallas kernels, on_device(): pl.pallas_call(functools.partial(assemble_kernel, n, groups, block, scale...  44.3 us
    pallas_call x1, Pallas kernels, on_device(): pl.pallas_call(functools.partial(finish_kernel, groups), grid=(count // b...  18.4 us
    unnamed x10, local copies, waits for them, and re-layouts  3.68 us

profile of v2, /device:TPU:0, one launch (start us, length us, event | category | flops | bytes accessed | tf_op | source)
XLA Modules:
  0.0 67.5 jit_solution(11539964731901021743)
XLA Ops:
  0.6 0.0 copy-start
  0.6 0.9 %copy-done = bf16[128,512]{1,0:T(8,128)(2,1)S(1)} copy-done((bf16[128,512]{1,0:T(8,128)(2,1)S(1)}, bf16[128,512]{1,0:T(8,128)(2,1)}, u32[]{:S(2)}) %copy-start) | copy-done | bytes 131096
  1.5 0.0 copy-start.1
  1.5 0.8 %copy-done.1 = bf16[1,128,128]{2,1,0:T(8,128)(2,1)S(1)} copy-done((bf16[1,128,128]{2,1,0:T(8,128)(2,1)S(1)}, bf16[1,128,128]{2,1,0:T(8,128)(2,1)}, u32[]{:S(2)}) %copy-start.1) | copy-done | bytes 32792
  2.3 0.0 copy-start.2
  2.3 0.7 %copy-done.2 = s32[1,128,16]{1,2,0:T(8,128)S(1)} copy-done((s32[1,128,16]{1,2,0:T(8,128)S(1)}, s32[1,128,16]{1,2,0:T(8,128)}, u32[]{:S(2)}) %copy-start.2) | copy-done | bytes 8216
  3.0 0.0 copy-start.3
  3.0 0.7 %copy-done.3 = f32[256]{0:T(256)S(1)} copy-done((f32[256]{0:T(256)S(1)}, f32[256]{0:T(256)}, u32[]{:S(2)}) %copy-start.3) | copy-done | bytes 1048
  3.7 0.0 copy-start.4
  3.7 0.7 copy-done.4
  4.3 44.3 %assemble.1 = (bf16[2048,512]{1,0:T(8,128)(2,1)S(1)}, bf16[256,512]{1,0:T(8,128)(2,1)S(1)}, bf16[256,512]{1,0:T(8,128)(2,1)S(1)}, f32[2,128]{1,0:T(2,128)S(1)}) custom-call(s32[1,16]{1,0:T(1,128)S(1)} %bitcast.14, s32[2048]{0:T(1024)S(1)} %bitcast.11, bf16[128,128]{1,0:T(8,128)(2,1)S(1)} %bitcast.10, bf16[128,512]{1,0:T(8,128)(2,1)S(1)} %copy-done, ...), custom_call_target="tpu_custom_call" | custom-call | tf_op jit(solution)/shard_map/assemble/pallas_call | solution.py:402
  48.6 18.4 %finish.1 = (f32[4096,128]{1,0:T(8,128)}, f32[8,128]{1,0:T(8,128)S(1)}) custom-call(s32[16]{0:T(128)S(1)} %copy-done.4, bf16[2048,512]{1,0:T(8,128)(2,1)S(1)} %get-tuple-element.8.slab_ref, bf16[256,512]{1,0:T(8,128)(2,1)S(1)} %get-tuple-element.9.column_ref, bf16[256,512]{1,0:T(8,128)(2,1)S(1)} %get-tuple-element.10.fp_ref, ...), custom_call_target="tpu_custom_call" | custom-call | tf_op jit(solution)/shard_map/finish/pallas_call | solution.py:427
  67.0 0.5 slice.3
Async XLA Ops:
  0.6 0.9 %copy-start = (bf16[128,512]{1,0:T(8,128)(2,1)S(1)}, bf16[128,512]{1,0:T(8,128)(2,1)}, u32[]{:S(2)}) copy-start(bf16[128,512]{1,0:T(8,128)(2,1)} %w_ref.1) | copy-start | bytes 393220
  1.5 0.8 %copy-start.1 = (bf16[1,128,128]{2,1,0:T(8,128)(2,1)S(1)}, bf16[1,128,128]{2,1,0:T(8,128)(2,1)}, u32[]{:S(2)}) copy-start(bf16[1,128,128]{2,1,0:T(8,128)(2,1)} %param.5) | copy-start | bytes 98308
  2.3 0.7 %copy-start.2 = (s32[1,128,16]{1,2,0:T(8,128)S(1)}, s32[1,128,16]{1,2,0:T(8,128)}, u32[]{:S(2)}) copy-start(s32[1,128,16]{1,2,0:T(8,128)} %param.6) | copy-start | bytes 24580
  3.0 0.7 %copy-start.3 = (f32[256]{0:T(256)S(1)}, f32[256]{0:T(256)}, u32[]{:S(2)}) copy-start(f32[256]{0:T(256)} %param.8) | copy-start | bytes 3076
  3.7 0.7 copy-start.4

commit v3 on v2

--- a/solution.py
+++ b/solution.py
@@ -107,6 +107,55 @@
     return drain
 
 
+def short_gather(n, me, buf, rows, pieces, send_sem, recv_sem):
+    depth = n // 4
+    z, y, x = me // 4, (me // 2) % 2, me % 2
+    xn = me + 1 - 2 * x
+    yn = me + 2 - 4 * y
+    corners = (xn, yn, xn + 2 - 4 * y)
+    whole = (0, sum(size for _, size in pieces))
+
+    def line(base, turn):
+        return base % 4 + lax.rem(z + turn, depth) * 4
+
+    def copy(origin, sem, target):
+        block = slots(buf, origin, rows, whole)
+        return pltpu.make_async_remote_copy(
+            src_ref=block,
+            dst_ref=block,
+            send_sem=send_sem.at[sem],
+            recv_sem=recv_sem.at[origin],
+            device_id={"band": target},
+            device_id_type=MESH,
+        )
+
+    sent = []
+
+    def send(origin, target):
+        item = copy(origin, len(sent), target)
+        item.start()
+        sent.append(item)
+
+    for turn in range(1, depth):
+        send(me, line(me, turn))
+    for corner in corners:
+        send(me, corner)
+    for turn in range(1, depth):
+        origin = line(me, depth - turn)
+        copy(origin, 0, me).wait_recv()
+        for corner in corners:
+            send(origin, corner)
+    for turn in range(depth):
+        for corner in corners:
+            copy(line(corner, turn), 0, me).wait_recv()
+
+    def drain():
+        for item in sent:
+            item.wait_send()
+
+    return drain
+
+
 def direct_gather(n, me, buf, rows, pieces, send_sem, recv_sem, make=None):
     whole = (0, sum(size for _, size in pieces))
 
@@ -143,15 +192,15 @@
 
 def assemble_kernel(
     n, groups, block, scale,
-    order_ref, nbrs_ref, feats_ref, w_ref, stiff_ref,
-    slab_ref, column_ref, pivot_ref, pstiff_ref,
-    gathered, wide, near, pivots,
+    order_hbm, nbrs_hbm, feats_hbm, w_hbm, stiff_hbm,
+    slab_ref, column_ref, pivot_ref, pstiff_ref, stiff_ref, chosen_ref,
+    order_ref, nbrs_ref, w_ref, load_sem, gathered, wide, near, pivots,
     fsend, frecv, ssend, srecv, csend, crecv, psend, precv,
 ):
     me = lax.axis_index("band")
     slab = lax.axis_index("slab")
-    beads = feats_ref.shape[0]
-    links = nbrs_ref.shape[0] // beads
+    beads = feats_hbm.shape[0]
+    links = nbrs_hbm.shape[0] // beads
     frows = beads + TAIL
     tree = n == 16
     gather = tree_gather if tree else direct_gather
@@ -160,12 +209,11 @@
 
     barrier = pltpu.get_barrier_semaphore()
     if tree:
-        z, y, x = me // 4, (me // 2) % 2, me % 2
-        mates = [(me + 1 - 2 * x, None), (me + 2 - 4 * y, None), (me + 4, z < n // 4 - 1), (me - 4, z > 0)]
-        for mate, cond in mates:
-            def greet(mate=mate):
-                pl.semaphore_signal(barrier, inc=1, device_id={"band": mate}, device_id_type=MESH)
-            greet() if cond is None else pl.when(cond)(greet)
+        y, x = (me // 2) % 2, me % 2
+        xn, yn = me + 1 - 2 * x, me + 2 - 4 * y
+        mates = [xn, yn, xn + 2 - 4 * y] + [lax.rem(me + 4 * turn, n) for turn in range(1, n // 4)]
+        for mate in mates:
+            pl.semaphore_signal(barrier, inc=1, device_id={"band": mate}, device_id_type=MESH)
     else:
         @pl.loop(1, n)
         def _(shift):
@@ -174,7 +222,19 @@
         pl.semaphore_signal(barrier, inc=1, device_id={"slab": lax.rem(slab + shift, groups)}, device_id_type=MESH)
 
     mine = pl.multiple_of(me * frows, 16)
-    gathered[pl.ds(mine, beads), :] = feats_ref[...]
+    loads = [
+        pltpu.make_async_copy(source, target, load_sem.at[i])
+        for i, (source, target) in enumerate((
+            (stiff_hbm, stiff_ref),
+            (feats_hbm, gathered.at[pl.ds(mine, beads), :]),
+            (nbrs_hbm, nbrs_ref),
+            (w_hbm, w_ref),
+            (order_hbm, order_ref),
+        ))
+    ]
+    for load in loads:
+        load.start()
+    loads[0].wait()
     stiff = stiff_ref[...]
     high = stiff.astype(jnp.bfloat16).astype(jnp.float32)
     mid = (stiff - high).astype(jnp.bfloat16).astype(jnp.float32)
@@ -182,15 +242,17 @@
     parts = jnp.concatenate([high, mid, low], axis=0)
     tail = jnp.concatenate([parts, jnp.zeros((TAIL - parts.shape[0], parts.shape[1]), jnp.float32)], axis=0)
     gathered[pl.ds(mine + beads, TAIL), :] = tail.astype(jnp.bfloat16)
+    loads[1].wait()
 
     if tree:
-        inner = jnp.logical_and(z > 0, z < n // 4 - 1)
-        pl.semaphore_wait(barrier, jnp.where(inner, groups + 3, groups + 2))
+        pl.semaphore_wait(barrier, len(mates) + groups - 1)
     else:
         pl.semaphore_wait(barrier, n - 1 + groups - 1)
 
     half = beads // 2
-    drain_feats = gather(n, me, gathered, frows, ((0, half), (half, half + TAIL)), fsend, frecv)
+    drain_feats = (short_gather if tree else direct_gather)(n, me, gathered, frows, ((0, half), (half, half + TAIL)), fsend, frecv)
+    for load in loads[2:]:
+        load.wait()
     for origin in range(n):
         wide[pl.ds(origin * beads, beads), :] = gathered[pl.ds(origin * frows, beads), :].astype(jnp.float32)
 
@@ -205,7 +267,7 @@
                 for bead in range(chunk):
                     row = nbrs_ref[link * beads + base + bead]
                     near[pl.ds(link * chunk + bead, 1), :] = wide[pl.ds(row, 1), :]
-            own = feats_ref[pl.ds(base, chunk), :].astype(jnp.float32)
+            own = gathered[pl.ds(pl.multiple_of(mine + base, 16), chunk), :].astype(jnp.float32)
             mixed = near[...].reshape(links, chunk, -1) * own[None]
             mixed = mixed.reshape(links * chunk, -1).astype(jnp.bfloat16)
             pre = jnp.dot(mixed, w_ref[...], preferred_element_type=jnp.float32)
@@ -215,6 +277,7 @@
     drain_slab = gather(n, me, slab_ref, beads, ((0, half), (half, half)), ssend, srecv, make)
 
     chosen = order_ref[:, 0:1]
+    chosen_ref[...] = jnp.broadcast_to(chosen, chosen_ref.shape)
     blocks = slab_ref.shape[0] // block
     passed = [(chosen >= (r + 1) * groups).astype(jnp.int32) for r in range(blocks)]
     number = sum(passed)
@@ -343,17 +406,17 @@
         change = dot3(done[:, :block - low], done, ((0,), (0,)))
         work[low:, low:] = work[low:, low:] - change[:, :block - low]
         ident[low:, :high] = ident[low:, :high] - change[:, block - low:]
-    log_ref[...] = jnp.broadcast_to(logs * (1.0 / (STEPS * block)), log_ref.shape)
+    log_ref[0, 0] = jnp.sum(logs) * (1.0 / (STEPS * block))
 
 
 def finish_kernel(
-    groups, order_ref, slab_ref, column_ref, fp_ref, pstiff_ref, stiff_ref,
+    groups, chosen_ref, slab_ref, column_ref, fp_ref, pstiff_ref, stiff_ref,
     out_ref, log_ref, work, ident, lowinv, whigh, wlow, pcol,
 ):
     me = lax.axis_index("band")
     slab = lax.axis_index("slab")
     r = pl.program_id(0)
-    pivot = order_ref[0]
+    pivot = chosen_ref[...]
     block = fp_ref.shape[0]
     nt = (((1,), (1,)), ((), ()))
 
@@ -397,19 +460,25 @@
     stiff2 = stiff.reshape(block // 128, 128)
     scale = 1.5 / math.sqrt(links * channels)
     vmem = pl.BlockSpec(memory_space=pltpu.VMEM)
-    smem = pl.BlockSpec(memory_space=pltpu.SMEM)
+    hbm = pl.BlockSpec(memory_space=pltpu.HBM)
     dma = pltpu.SemaphoreType.DMA
-    slab_factor, column, pivot_factor, pivot_stiff = pl.pallas_call(
+    slab_factor, column, pivot_factor, pivot_stiff, own_stiff, chosen = pl.pallas_call(
         functools.partial(assemble_kernel, n, groups, block, scale),
         out_shape=(
             jax.ShapeDtypeStruct((count, channels), jnp.bfloat16),
             jax.ShapeDtypeStruct((block, channels), jnp.bfloat16),
             jax.ShapeDtypeStruct((block, channels), jnp.bfloat16),
             jax.ShapeDtypeStruct((block // 128, 128), jnp.float32),
+            jax.ShapeDtypeStruct((block // 128, 128), jnp.float32),
+            jax.ShapeDtypeStruct((1, block), jnp.int32),
         ),
-        in_specs=[vmem, smem, vmem, vmem, vmem],
-        out_specs=(vmem, vmem, vmem, vmem),
+        in_specs=[hbm] * 5,
+        out_specs=(vmem,) * 6,
         scratch_shapes=[
+            pltpu.VMEM((1, order.shape[0]), jnp.int32),
+            pltpu.SMEM((links * beads,), jnp.int32),
+            pltpu.VMEM((width, channels), jnp.bfloat16),
+            dma((5,)),
             pltpu.VMEM((n * (beads + TAIL), width), jnp.bfloat16),
             pltpu.VMEM((count, width), jnp.float32),
             pltpu.VMEM((links * 16, width), jnp.float32),
@@ -418,7 +487,7 @@
             dma((groups,)), dma(()), dma((groups,)), dma((groups,)),
         ],
         compiler_params=pltpu.CompilerParams(
-            collective_id=0, has_side_effects=True, vmem_limit_bytes=32 * 1024 * 1024
+            collective_id=0, has_side_effects=True, vmem_limit_bytes=60 * 1024 * 1024
         ),
         name="assemble",
     )(order.reshape(1, -1), flat, own_feats, w_pair, stiff2)
@@ -429,17 +498,17 @@
         grid=(count // block,),
         out_shape=(
             jax.ShapeDtypeStruct((count * block // 128, 128), jnp.float32),
-            jax.ShapeDtypeStruct((8, 128), jnp.float32),
+            jax.ShapeDtypeStruct((1, 1), jnp.float32),
         ),
         in_specs=[
-            smem,
+            whole((1, block)),
             pl.BlockSpec((block, channels), lambda r: (r, 0)),
             whole((block, channels)), whole((block, channels)),
             whole((block // 128, 128)), whole((block // 128, 128)),
         ],
         out_specs=(
             pl.BlockSpec((block * block // 128, 128), lambda r: (r, 0)),
-            whole((8, 128)),
+            pl.BlockSpec(memory_space=pltpu.SMEM),
         ),
         scratch_shapes=[
             pltpu.VMEM((block, block), jnp.float32),
@@ -449,9 +518,9 @@
             pltpu.VMEM((block, channels), jnp.bfloat16),
             pltpu.VMEM((block, block), jnp.bfloat16),
         ],
-        compiler_params=pltpu.CompilerParams(vmem_limit_bytes=32 * 1024 * 1024),
+        compiler_params=pltpu.CompilerParams(vmem_limit_bytes=60 * 1024 * 1024),
         name="finish",
-    )(order, slab_factor, column, pivot_factor, pivot_stiff, stiff2)
+    )(chosen, slab_factor, column, pivot_factor, pivot_stiff, own_stiff)
     return out.reshape(1, count, 1, block), logs[0, 0]
 
 

time: 67.8 us -> 64.1 us (0.945)
  local copies, waits for them, and re-layouts: 4.2 us -> 0 us
    unnamed x10 -> x0, local copies, waits for them, and re-layouts: 3.68 us -> none
    pallas_call x1, Pallas kernels: 18.4 us -> 20 us  [on_device(): pl.pallas_call(functools.partial(finish_kernel, groups), grid=(count // b...]
    pallas_call x1, Pallas kernels: 44.3 us -> 43.1 us  [on_device(): pl.pallas_call(functools.partial(assemble_kernel, n, groups, block, scale...]
where the time goes in v3:
time: 64.1 us; the launch traced here: 63.8 us
  Pallas kernels  63.1 us (98%)
    pallas_call x1, Pallas kernels, on_device(): pl.pallas_call(functools.partial(assemble_kernel, n, groups, block, scale...  43.1 us
    pallas_call x1, Pallas kernels, on_device(): pl.pallas_call(functools.partial(finish_kernel, groups), grid=(count // b...  20 us

profile of v3, /device:TPU:0, one launch (start us, length us, event | category | flops | bytes accessed | tf_op | source)
XLA Modules:
  0.0 63.8 jit_solution(13518566934063821567)
XLA Ops:
  0.6 43.1 %assemble.1 = (bf16[2048,512]{1,0:T(8,128)(2,1)}, bf16[256,512]{1,0:T(8,128)(2,1)}, bf16[256,512]{1,0:T(8,128)(2,1)}, f32[2,128]{1,0:T(2,128)}, f32[2,128]{1,0:T(2,128)}, /*index=5*/s32[1,256]{1,0:T(1,128)}) custom-call(s32[1,16]{1,0:T(1,128)} %bitcast.13, s32[2048]{0:T(1024)} %bitcast.11, bf16[128,128]{1,0:T(8,128)(2,1)} %bitcast.10, ...), custom_call_target="tpu_custom_call" | custom-call | tf_op jit(solution)/shard_map/assemble/pallas_call | solution.py:465
  43.7 20.0 %finish.1 = (f32[4096,128]{1,0:T(8,128)}, f32[1,1]{1,0:T(1,128)}) custom-call(s32[1,256]{1,0:T(1,128)} %get-tuple-element.10.chosen_ref, bf16[2048,512]{1,0:T(8,128)(2,1)} %get-tuple-element.11.slab_ref, bf16[256,512]{1,0:T(8,128)(2,1)} %get-tuple-element.12.column_ref, bf16[256,512]{1,0:T(8,128)(2,1)} %get-tuple-element.13.fp_ref, ...), custom_call_target="tpu_custom_call" | custom-call | tf_op jit(solution)/shard_map/finish/pallas_call | solution.py:496

commit v4 on v3

--- a/solution.py
+++ b/solution.py
@@ -276,6 +276,20 @@
 
     drain_slab = gather(n, me, slab_ref, beads, ((0, half), (half, half)), ssend, srecv, make)
 
+    home_rows = pl.ds(pl.multiple_of(home * block, 16), block)
+
+    def column_copy(shift):
+        return pltpu.make_async_remote_copy(
+            src_ref=slab_ref.at[home_rows, :], dst_ref=column_ref, send_sem=csend.at[shift], recv_sem=crecv,
+            device_id={"slab": lax.rem(slab + shift, groups)}, device_id_type=MESH,
+        )
+
+    @pl.when(slab == owner)
+    def _():
+        for shift in range(1, groups):
+            column_copy(shift).start()
+        column_ref[...] = slab_ref[home_rows, :]
+
     chosen = order_ref[:, 0:1]
     chosen_ref[...] = jnp.broadcast_to(chosen, chosen_ref.shape)
     blocks = slab_ref.shape[0] // block
@@ -301,24 +315,6 @@
 
     for shift in range(1, groups):
         pivot_copy(shift, slab).start()
-
-    def column_copy(shift):
-        return pltpu.make_async_remote_copy(
-            src_ref=column_ref, dst_ref=column_ref, send_sem=csend.at[shift], recv_sem=crecv,
-            device_id={"slab": lax.rem(slab + shift, groups)}, device_id_type=MESH,
-        )
-
-    @pl.when(slab == owner)
-    def _():
-        column_ref[...] = slab_ref[pl.ds(pl.multiple_of(home * block, 16), block), :]
-        for shift in range(1, groups):
-            column_copy(shift).start()
-        for shift in range(1, groups):
-            column_copy(shift).wait_send()
-
-    @pl.when(slab != owner)
-    def _():
-        column_copy(1).wait_recv()
 
     for shift in range(1, groups):
         pivot_copy(shift, lax.rem(slab + groups - shift, groups)).wait_recv()
@@ -337,6 +333,16 @@
 
     for shift in range(1, groups):
         pivot_copy(shift, slab).wait_send()
+
+    @pl.when(slab != owner)
+    def _():
+        column_copy(1).wait_recv()
+
+    @pl.when(slab == owner)
+    def _():
+        for shift in range(1, groups):
+            column_copy(shift).wait_send()
+
     drain_feats()
     drain_slab()
 

time: 64.1 us -> 63.8 us (level)
  no operation moved by 1% of the time
where the time goes in v4:
time: 63.8 us; the launch traced here: 63.4 us
  Pallas kernels  62.8 us (98%)
  between operations  0.64 us (1%)
    pallas_call x1, Pallas kernels, on_device(): pl.pallas_call(functools.partial(assemble_kernel, n, groups, block, scale...  42.8 us
    pallas_call x1, Pallas kernels, on_device(): pl.pallas_call(functools.partial(finish_kernel, groups), grid=(count // b...  20 us

profile of v4, /device:TPU:0, one launch (start us, length us, event | category | flops | bytes accessed | tf_op | source)
XLA Modules:
  0.0 63.4 jit_solution(10661351151276820472)
XLA Ops:
  0.6 42.8 %assemble.1 = (bf16[2048,512]{1,0:T(8,128)(2,1)}, bf16[256,512]{1,0:T(8,128)(2,1)}, bf16[256,512]{1,0:T(8,128)(2,1)}, f32[2,128]{1,0:T(2,128)}, f32[2,128]{1,0:T(2,128)}, /*index=5*/s32[1,256]{1,0:T(1,128)}) custom-call(s32[1,16]{1,0:T(1,128)} %bitcast.13, s32[2048]{0:T(1024)} %bitcast.11, bf16[128,128]{1,0:T(8,128)(2,1)} %bitcast.10, ...), custom_call_target="tpu_custom_call" | custom-call | tf_op jit(solution)/shard_map/assemble/pallas_call | solution.py:471
  43.4 20.0 %finish.1 = (f32[4096,128]{1,0:T(8,128)}, f32[1,1]{1,0:T(1,128)}) custom-call(s32[1,256]{1,0:T(1,128)} %get-tuple-element.10.chosen_ref, bf16[2048,512]{1,0:T(8,128)(2,1)} %get-tuple-element.11.slab_ref, bf16[256,512]{1,0:T(8,128)(2,1)} %get-tuple-element.12.column_ref, bf16[256,512]{1,0:T(8,128)(2,1)} %get-tuple-element.13.fp_ref, ...), custom_call_target="tpu_custom_call" | custom-call | tf_op jit(solution)/shard_map/finish/pallas_call | solution.py:502
